TPU v7x, 32 devices: a whole 2x2x4 slice. The times are simulated.
32 devices in a mesh: groups: 2 (over x), row: 16 (over z, y, core).
Axes of the slice: x: 2, y: 2, z: 4, core: 2. Of those that a mesh axis runs over, the one named last changes fastest.
Arguments:
- normals: bfloat16 [128, 32768], P('groups', 'row'), parts along dimension 0, may hold values from -6 to 6
- variance: float32 [65536], P(('groups', 'row')), parts along dimension 0, may hold values from 0.3 to 3
- tiles: bfloat16 [640, 512, 512], P(('groups', 'row')), parts along dimension 0, may hold values from -0.078125 to 0.078125
- tile_ids: int32 [640, 2], P(('groups', 'row')), parts along dimension 0, may hold values from -1 to 63, as said below
Outputs:
- lanczos_basis: float32 [4, 128, 32768], P(None, 'groups', 'row'), parts along dimension 1
- alphas: float32 [3, 128], P(None, 'groups'), parts along dimension 1
- betas: float32 [3, 128], P(None, 'groups'), parts along dimension 1
There are 2 independent parts, one for each index of `groups`. A program takes and returns all parts, laid end to end along the dimension named above; each array names one. Nothing has to cross between parts.
Inputs may be any that keep to these rules, and one draw needn't show every extreme that they name: `tile_ids`: on the device at index d of row, every used slot holds a tile row i among d * 4 .. d * 4 + 3 and a tile column j with i - 4 <= j <= i, j >= 0; each pair appears at most once in a part; every diagonal pair (i, i) appears; an unused slot holds -1 in both entries; in every draw some device uses all 20 slots.
All inputs are finite; a program needn't handle non-finite values.
Results may differ from a plain program's by a relative error of at most 0.0059.
Values may be sent and summed in bfloat16 or wider, within the bound.
A program may use at most 128 MiB of HBM per device.

v0:
```python
import math

import jax
import jax.numpy as jnp
from jax import lax
from jax.sharding import PartitionSpec as P

ITERS = 3


def passed_along(value, axis, steps):
    count = lax.axis_size(axis)
    leading, last = (max(0, -steps), min(count, count - steps))
    return lax.ppermute(value, axis, [(source, source + steps) for source in range(leading, last)])


def build_blocks(tiles, tile_ids, first_block, block_count, tile_width):
    span = block_count * tile_width
    empty = jnp.zeros((span, span), tiles.dtype)

    def place_tile(slot, carried):
        own_block, cross_block = carried
        tile_val = lax.dynamic_index_in_dim(tiles, slot, 0, keepdims=False)
        slot_ids = lax.dynamic_index_in_dim(tile_ids, slot, 0, keepdims=False)
        is_live = slot_ids[0] >= 0
        row_local = jnp.clip(slot_ids[0] - first_block, 0, block_count - 1)
        col_local = slot_ids[1] - first_block
        in_own = col_local >= 0
        col_pos = jnp.clip(
            jnp.where(in_own, col_local, col_local + block_count), 0, block_count - 1
        )
        row_start = row_local * tile_width
        col_start = col_pos * tile_width
        old_own = lax.dynamic_slice(own_block, (row_start, col_start), (tile_width, tile_width))
        new_own = jnp.where(is_live & in_own, tile_val, old_own)
        own_block = lax.dynamic_update_slice(own_block, new_own, (row_start, col_start))
        old_cross = lax.dynamic_slice(cross_block, (row_start, col_start), (tile_width, tile_width))
        new_cross = jnp.where(is_live & jnp.logical_not(in_own), tile_val, old_cross)
        cross_block = lax.dynamic_update_slice(cross_block, new_cross, (row_start, col_start))
        return (own_block, cross_block)

    return lax.fori_loop(0, tiles.shape[0], place_tile, (empty, empty))


def times_transpose(vq, block):
    return lax.dot_general(vq, block, (((1,), (1,)), ((), ())), preferred_element_type=jnp.float32)


def shards(normals, variance, tiles, tile_ids):
    row_count = variance.shape[0]
    tile_width = tiles.shape[1]
    block_count = row_count // tile_width
    first_block = lax.axis_index("row") * block_count
    own_block, cross_block = build_blocks(tiles, tile_ids, first_block, block_count, tile_width)
    draws_f = normals.astype(jnp.float32)
    norm_start = jnp.sqrt(lax.psum(jnp.sum(draws_f * draws_f, axis=1), "row"))
    vector = draws_f / norm_start[:, None]
    basis = [vector]
    alpha_list = []
    beta_list = []
    for levels in range(ITERS):
        vq = vector.astype(jnp.bfloat16)
        prev_piece = passed_along(vq, "row", 1)
        image_vec = variance[None, :] * vector
        image_vec = image_vec + times_transpose(vq, own_block)
        image_vec = image_vec + jnp.dot(vq, own_block, preferred_element_type=jnp.float32)
        image_vec = image_vec + times_transpose(prev_piece, cross_block)
        reaching = jnp.dot(vq, cross_block, preferred_element_type=jnp.float32)
        image_vec = image_vec + passed_along(reaching.astype(jnp.bfloat16), "row", -1).astype(
            reaching.dtype
        )
        stacked = jnp.stack(basis)
        local_proj = jnp.sum(stacked * image_vec[None], axis=2)
        proj = lax.psum(local_proj, "row")
        image_vec = image_vec - jnp.sum(stacked * proj[:, :, None], axis=0)
        sq_total = lax.psum(jnp.sum(image_vec * image_vec, axis=1), "row")
        beta_now = jnp.sqrt(sq_total + 1e-06)
        vector = image_vec / beta_now[:, None]
        alpha_list.append(proj[levels])
        beta_list.append(beta_now)
        basis.append(vector)
    scale_factor = math.sqrt(row_count * lax.axis_size("row"))
    return (jnp.stack(basis) * scale_factor, jnp.stack(alpha_list), jnp.stack(beta_list))


def solution(mesh):
    return jax.shard_map(
        shards,
        mesh=mesh,
        in_specs=(
            P("groups", "row"),
            P(("groups", "row")),
            P(("groups", "row"), None, None),
            P(("groups", "row"), None),
        ),
        out_specs=(P(None, "groups", "row"), P(None, "groups"), P(None, "groups")),
        check_vma=False,
    )
```

profile of v0, /device:TPU:0, one launch (start us, length us, event | category | flops | bytes accessed | tf_op | source)
XLA Modules:
  0.0 385.4 jit_solution(15279335730251632674)
XLA Ops:
  0.6 4.3 %broadcast_in_dim.2 = bf16[2048,2048]{1,0:T(8,128)(2,1)} broadcast(bf16[]{:T(256)} %constant.64.clone.1), dimensions={} | broadcast | bytes 8388610 | tf_op jit(solution)/shard_map/broadcast_in_dim | solution.py:19
  4.9 4.3 %broadcast_in_dim.2.clone = bf16[2048,2048]{1,0:T(8,128)(2,1)} broadcast(bf16[]{:T(256)} %constant.64.clone.1), dimensions={} | broadcast | bytes 8388610 | tf_op jit(solution)/shard_map/broadcast_in_dim | solution.py:19
  9.2 100.8 %while.15 = (s32[]{:T(128)}, bf16[2048,2048]{1,0:T(8,128)(2,1)}, bf16[2048,2048]{1,0:T(8,128)(2,1)}, s32[20,2]{0,1:T(2,128)S(1)}, s32[]{:T(128)}, /*index=5*/bf1...) while((s32[]{:T(128)}, bf16[2048,2048]{1,0:T(8,128)(2,1)}, ...), condition=%wide.region_3.4_spmd, body=%wide.region_2.3_spmd.sunk | while | flops 524311 | bytes 2622330 | solution.py:42
  11.6 2.6 fusion.44
  16.6 2.7 fusion.44
  21.7 2.6 fusion.44
  26.7 2.6 fusion.44
  31.7 2.7 fusion.44
  36.8 2.6 fusion.44
  41.8 2.7 fusion.44
  46.8 2.7 fusion.44
  51.9 2.7 fusion.44
  56.9 2.7 fusion.44
  62.0 2.7 fusion.44
  67.0 2.6 fusion.44
  72.0 2.7 fusion.44
  77.1 2.7 fusion.44
  82.2 2.7 fusion.44
  87.2 2.7 fusion.44
  92.3 2.6 fusion.44
  97.3 2.6 fusion.44
  102.3 2.7 fusion.44
  107.4 2.6 fusion.44
  110.1 34.5 %psum.49 = f32[64]{0:T(128)S(1)} all-reduce(f32[64]{0:T(128)S(1)} %fusion.5), channel_id=1, replica_groups=mesh['groups'=2,'row'=16] {'row'}, use_global_device_ids=true, to_apply=%region_1.2 | all-reduce | flops 64 | bytes 512 | tf_op jit(solution)/shard_map/psum | solution.py:56
  144.6 5.2 %convolution_convert_fusion.2 = bf16[64,2048]{1,0:T(8,128)(2,1)S(1)} fusion(bf16[2048,2048]{1,0:T(8,128)(2,1)} %get-tuple-element.114, f32[64]{0:T(128)S(1)} %sqrt.12, bf16[64,2048]{1,0:T(8,128)(2,1)S(1)} %copy-done.1), kind=kOutput, calls=%fused_computation.17 | convolution fusion | flops 537395200 | bytes 8913152 | tf_op jit(solution)/shard_map/dot_general | solution.py:68
  149.8 1.3 collective-permute-start.1
  151.2 3.0 collective-permute-start
  154.3 2.7 convolution_add_fusion.6
  157.0 1.6 convolution_add_fusion.5
  159.2 2.8 multiply_reduce_fusion.7
  162.0 29.5 %psum.50 = f32[1,64]{1,0:T(1,128)S(1)} all-reduce(f32[1,64]{1,0:T(1,128)S(1)} %bitcast.68), channel_id=1, replica_groups=mesh['groups'=2,'row'=16] {'row'}, use_global_device_ids=true, to_apply=%region_5.6 | all-reduce | flops 64 | bytes 512 | tf_op jit(solution)/shard_map/psum | solution.py:74
  191.8 29.5 %psum.51 = f32[64]{0:T(128)S(1)} all-reduce(f32[64]{0:T(128)S(1)} %multiply_reduce_fusion.6), channel_id=1, replica_groups=mesh['groups'=2,'row'=16] {'row'}, use_global_device_ids=true, to_apply=%region_7.8 | all-reduce | flops 64 | bytes 512 | tf_op jit(solution)/shard_map/psum | solution.py:76
  221.5 5.1 %convolution_convert_fusion.1 = bf16[64,2048]{1,0:T(8,128)(2,1)S(1)} fusion(bf16[64,2048]{1,0:T(8,128)(2,1)S(1)} %get-tuple-element.131, bf16[2048,2048]{1,0:T(8,128)(2,1)} %get-tuple-element.114), kind=kOutput, calls=%fused_computation.16 | convolution fusion | flops 537001984 | bytes 8912896 | tf_op jit(solution)/shard_map/dot_general | solution.py:68
  227.3 2.6 fusion.18
  230.0 2.2 collective-permute-start.2
  232.2 1.3 collective-permute-start.3
  233.5 1.6 convolution_add_fusion.3
  235.7 2.7 fusion.3
  238.5 33.7 %psum.52 = f32[2,64]{1,0:T(2,128)S(1)} all-reduce(f32[2,64]{1,0:T(2,128)S(1)} %multiply_reduce_fusion.3), channel_id=1, replica_groups=mesh['groups'=2,'row'=16] {'row'}, use_global_device_ids=true, to_apply=%region_9.10 | all-reduce | flops 128 | bytes 1024 | tf_op jit(solution)/shard_map/psum | solution.py:74
  272.5 29.5 %psum.53 = f32[64]{0:T(128)S(1)} all-reduce(f32[64]{0:T(128)S(1)} %get-tuple-element.129), channel_id=1, replica_groups=mesh['groups'=2,'row'=16] {'row'}, use_global_device_ids=true, to_apply=%region_12.13 | all-reduce | flops 64 | bytes 512 | tf_op jit(solution)/shard_map/psum | solution.py:76
  302.2 5.1 %convolution_convert_fusion = bf16[64,2048]{1,0:T(8,128)(2,1)S(1)} fusion(bf16[64,2048]{1,0:T(8,128)(2,1)S(1)} %get-tuple-element.138, bf16[2048,2048]{1,0:T(8,128)(2,1)} %get-tuple-element.114), kind=kOutput, calls=%fused_computation.15 | convolution fusion | flops 537001984 | bytes 8912896 | tf_op jit(solution)/shard_map/dot_general | solution.py:68
  308.0 2.6 fusion.19
  310.7 2.0 collective-permute-start.4
  314.0 1.6 convolution_add_fusion.1
  316.2 2.7 fusion.2
  319.1 33.7 %psum.54 = f32[3,64]{1,0:T(4,128)S(1)} all-reduce(f32[3,64]{1,0:T(4,128)S(1)} %multiply_reduce_fusion.1), channel_id=1, replica_groups=mesh['groups'=2,'row'=16] {'row'}, use_global_device_ids=true, to_apply=%region_14.15 | all-reduce | flops 192 | bytes 1536 | tf_op jit(solution)/shard_map/psum | solution.py:74
  353.1 29.5 %psum.55 = f32[64]{0:T(128)S(1)} all-reduce(f32[64]{0:T(128)S(1)} %get-tuple-element.127), channel_id=1, replica_groups=mesh['groups'=2,'row'=16] {'row'}, use_global_device_ids=true, to_apply=%region_17.18 | all-reduce | flops 64 | bytes 512 | tf_op jit(solution)/shard_map/psum | solution.py:76
  382.8 1.5 maximum_multiply_fusion
  (100 shorter events, 19.3 us)
Async XLA Ops:
  0.6 8.6 %copy-start.3 = (s32[20,2]{0,1:T(2,128)S(1)}, s32[20,2]{0,1:T(2,128)}, u32[]{:S(2)}) copy-start(s32[20,2]{0,1:T(2,128)} %param.9) | copy-start | bytes 484
  9.2 100.8 %copy-start.1 = (bf16[64,2048]{1,0:T(8,128)(2,1)S(1)}, bf16[64,2048]{1,0:T(8,128)(2,1)}, u32[]{:S(2)}) copy-start(bf16[64,2048]{1,0:T(8,128)(2,1)} %param.6) | copy-start | bytes 786436
  144.6 9.7 %copy-start = (bf16[2048,2048]{1,0:T(8,128)(2,1)S(1)}, bf16[2048,2048]{1,0:T(8,128)(2,1)}, u32[]{:S(2)}) copy-start(bf16[2048,2048]{1,0:T(8,128)(2,1)} %get-tuple-element.113) | copy-start | bytes 25165828
  144.6 9.7 %copy-start.2 = (f32[2048]{0:T(1024)S(1)}, f32[2048]{0:T(1024)}, u32[]{:S(2)}) copy-start(f32[2048]{0:T(1024)} %param.7) | copy-start | bytes 24580
  149.8 8.9 %collective-permute-start.1 = (bf16[64,2048]{1,0:T(8,128)(2,1)S(1)}, bf16[64,2048]{1,0:T(8,128)(2,1)S(1)}, u32[]{:S(2)}, u32[]{:S(2)}) collective-permute-start(bf16[64,2048]{1,0:T(8,128)(2,1)S(1)} %convolution_convert_fusion.2), channel_id=1, source_target_pairs={{1,0},{2,1},{3,2},{4,3},{5,4},{6,5},{7,6},{8,7},{9,8},{10,9},{11,1... | collective-permute-start | bytes 786440 | tf_op jit(solution)/shard_map/ppermute | solution.py:14
  151.2 7.5 %collective-permute-start = (bf16[64,2048]{1,0:T(8,128)(2,1)S(1)}, bf16[64,2048]{1,0:T(8,128)(2,1)S(1)}, u32[]{:S(2)}, u32[]{:S(2)}) collective-permute-start(bf16[64,2048]{1,0:T(8,128)(2,1)S(1)} %get-tuple-element.140), channel_id=1, source_target_pairs={{0,1},{1,2},{2,3},{3,4},{4,5},{5,6},{6,7},{7,8},{8,9},{9,10},{10,1... | collective-permute-start | bytes 786440 | tf_op jit(solution)/shard_map/ppermute | solution.py:14
  154.3 4.4 %slice-start = ((s8[8388608]{0:T(1024)(128)(4,1)}), s8[4194304]{0:T(1024)(128)(4,1)S(1)}, s32[]{:S(2)}) async-start(s8[8388608]{0:T(1024)(128)(4,1)} %bitcast.51), calls=%async_computation | async-start | bytes 8388608
  157.0 2.2 slice-start.1
  221.5 5.1 %slice-start.6 = ((s8[8388608]{0:T(1024)(128)(4,1)}), s8[4194304]{0:T(1024)(128)(4,1)S(1)}, s32[]{:S(2)}) async-start(s8[8388608]{0:T(1024)(128)(4,1)} %bitcast.57), calls=%async_computation.6 | async-start | bytes 8388608
  221.5 5.8 %slice-start.7 = ((s8[8388608]{0:T(1024)(128)(4,1)}), s8[4194304]{0:T(1024)(128)(4,1)S(1)}, s32[]{:S(2)}) async-start(s8[8388608]{0:T(1024)(128)(4,1)} %bitcast.57), calls=%async_computation.7 | async-start | bytes 8388608
  230.0 5.7 %slice-start.2 = ((s8[8388608]{0:T(1024)(128)(4,1)}), s8[4194304]{0:T(1024)(128)(4,1)S(1)}, s32[]{:S(2)}) async-start(s8[8388608]{0:T(1024)(128)(4,1)} %bitcast.53), calls=%async_computation.2 | async-start | bytes 8388608
  230.0 5.7 %collective-permute-start.2 = (bf16[64,2048]{1,0:T(8,128)(2,1)S(1)}, bf16[64,2048]{1,0:T(8,128)(2,1)S(1)}, u32[]{:S(2)}, u32[]{:S(2)}) collective-permute-start(bf16[64,2048]{1,0:T(8,128)(2,1)S(1)} %get-tuple-element.131), channel_id=1, source_target_pairs={{0,1},{1,2},{2,3},{3,4},{4,5},{5,6},{6,7},{7,8},{8,9},{9,10},{10,1... | collective-permute-start | bytes 786440 | tf_op jit(solution)/shard_map/ppermute | solution.py:14
  232.2 3.4 collective-permute-start.3
  233.5 2.2 slice-start.3
  302.2 5.1 %slice-start.8 = ((s8[8388608]{0:T(1024)(128)(4,1)}), s8[4194304]{0:T(1024)(128)(4,1)S(1)}, s32[]{:S(2)}) async-start(s8[8388608]{0:T(1024)(128)(4,1)} %bitcast.59), calls=%async_computation.8 | async-start | bytes 8388608
  302.2 5.8 %slice-start.9 = ((s8[8388608]{0:T(1024)(128)(4,1)}), s8[4194304]{0:T(1024)(128)(4,1)S(1)}, s32[]{:S(2)}) async-start(s8[8388608]{0:T(1024)(128)(4,1)} %bitcast.59), calls=%async_computation.9 | async-start | bytes 8388608
  308.0 8.2 %slice-start.4 = ((s8[8388608]{0:T(1024)(128)(4,1)}), s8[4194304]{0:T(1024)(128)(4,1)S(1)}, s32[]{:S(2)}) async-start(s8[8388608]{0:T(1024)(128)(4,1)} %bitcast.55), calls=%async_computation.4 | async-start | bytes 8388608
  310.7 5.5 %slice-start.5 = ((s8[8388608]{0:T(1024)(128)(4,1)}), s8[4194304]{0:T(1024)(128)(4,1)S(1)}, s32[]{:S(2)}) async-start(s8[8388608]{0:T(1024)(128)(4,1)} %bitcast.55), calls=%async_computation.5 | async-start | bytes 8388608
  310.7 5.5 %collective-permute-start.4 = (bf16[64,2048]{1,0:T(8,128)(2,1)S(1)}, bf16[64,2048]{1,0:T(8,128)(2,1)S(1)}, u32[]{:S(2)}, u32[]{:S(2)}) collective-permute-start(bf16[64,2048]{1,0:T(8,128)(2,1)S(1)} %get-tuple-element.138), channel_id=1, source_target_pairs={{0,1},{1,2},{2,3},{3,4},{4,5},{5,6},{6,7},{7,8},{8,9},{9,10},{10,1... | collective-permute-start | bytes 786440 | tf_op jit(solution)/shard_map/ppermute | solution.py:14
  312.7 3.4 collective-permute-start.5
where the time goes:
time: 387 us; the launch traced here: 385 us
  blocking collectives  220 us (57%)
  other arithmetic  57.6 us (15%)
  matrix products  36.4 us (9%)
  loops' own time  36 us (9%)
  local copies, waits for them, and re-layouts  22.5 us (6%)
  starting transfers between devices  11.2 us (3%)
    psum x3, blocking collectives, shards(): proj = lax.psum(local_proj, 'row')  96.9 us
    psum x3, blocking collectives, shards(): sq_total = lax.psum(jnp.sum(image_vec * image_vec, axis=1), 'row')  88.5 us
    dynamic_update_slice x20, other arithmetic, place_tile(): lax.dynamic_update_slice(cross_block, new_cross, (row_start, col_start))  52.9 us
    another operation x1, loops' own time, build_blocks(): return lax.fori_loop(0, tiles.shape[0], place_tile, (empty, empty))  36 us
    psum x1, blocking collectives, shards(): norm_start = jnp.sqrt(lax.psum(jnp.sum(draws_f * draws_f, axis=1), 'row'))  34.5 us
    dot_general x6, matrix products, times_transpose(): lax.dot_general(vq, block, (((1,), (1,)), ((), ())), preferred_element_ty...  16.1 us
    dot_general x3, matrix products, shards(): reaching = jnp.dot(vq, cross_block, preferred_element_type=jnp.float32)  15.4 us
    ppermute x6, starting transfers between devices, passed_along(): lax.ppermute(value, axis, [(source, source + steps) for source in range(l...  11.2 us
  transfers between devices with their start and end apart: 6, of which 2 were waited for; matrix products, arithmetic and copies ran while one was open for 2% of the time, Pallas kernels for 0%

commit v1 on v0

v1 whole, which is shorter than its diff:
```python
import functools
import math

import jax
import jax.numpy as jnp
from jax import lax
from jax.experimental import pallas as pl
from jax.experimental.pallas import tpu as pltpu
from jax.sharding import PartitionSpec as P

ITERS = 3
EPS = 1e-06
LANES = 128


def dot(a, b, transposed):
    dims = (((1,), (1 if transposed else 0,)), ((), ()))
    return lax.dot_general(a, b, dims, preferred_element_type=jnp.float32)


def lane_sums(value):
    total = value[:, :LANES]
    for at in range(LANES, value.shape[1], LANES):
        total = total + value[:, at : at + LANES]
    return total


def as_row(first, second):
    stacked = jnp.concatenate([first, second], axis=0)
    return jnp.sum(jnp.transpose(stacked), axis=0, keepdims=True)


def as_columns(row):
    return jnp.transpose(jnp.broadcast_to(row, (LANES, LANES)))


def kernel(
    n, ids, normals, variance, tiles, basis_out, alphas, betas,
    tiles_v, vq, prev, reach_s, reach_r, basis, image, psend, precv, slot_map, live_map,
    tile_sem, halo_send, halo_recv, back_send, back_recv, msg_send, msg_recv, out_sem,
):
    me = lax.axis_index("row")
    slots, width, _ = tiles.shape
    vecs, sites = normals.shape
    blocks = sites // width
    band = blocks + 1

    def tile_copy(s):
        return pltpu.make_async_copy(tiles.at[s], tiles_v.at[s], tile_sem.at[s])

    for s in range(slots):
        tile_copy(s).start()

    barrier = pltpu.get_barrier_semaphore()

    def greet(o, carry):
        pl.semaphore_signal(
            barrier, inc=1, device_id={"row": lax.rem(me + o, n)}, device_id_type=pl.DeviceIdType.MESH
        )
        return carry

    lax.fori_loop(1, n, greet, 0)

    def block(at):
        return pl.ds(at * width, width)

    def wide(column):
        return jnp.concatenate([column] * (width // LANES), axis=1)

    def halo_copy(k):
        return pltpu.make_async_remote_copy(
            src_ref=vq.at[k], dst_ref=prev.at[k], send_sem=halo_send.at[k], recv_sem=halo_recv.at[k],
            device_id={"row": lax.rem(me + 1, n)}, device_id_type=pl.DeviceIdType.MESH,
        )

    def back_copy(k):
        return pltpu.make_async_remote_copy(
            src_ref=reach_s.at[k], dst_ref=reach_r.at[k], send_sem=back_send.at[k], recv_sem=back_recv.at[k],
            device_id={"row": lax.rem(me + n - 1, n)}, device_id_type=pl.DeviceIdType.MESH,
        )

    def send_message(e, message):
        psend[e] = message
        precv[e, me] = message

        def send(o, carry):
            pltpu.make_async_remote_copy(
                src_ref=psend.at[e], dst_ref=precv.at[e, me], send_sem=msg_send.at[e], recv_sem=msg_recv.at[e],
                device_id={"row": lax.rem(me + o, n)}, device_id_type=pl.DeviceIdType.MESH,
            ).start()
            return carry

        lax.fori_loop(1, n, send, 0)

    def total_message(e):
        everyone = precv.at[e, pl.ds(0, n - 1)]
        pltpu.make_async_copy(everyone, everyone, msg_recv.at[e]).wait()
        return jnp.sum(precv[e], axis=0)

    def finish_message(e):
        everyone = precv.at[e, pl.ds(0, n - 1)]
        pltpu.make_async_copy(everyone, everyone, msg_send.at[e]).wait()

    def message(*rows):
        pad = jnp.zeros((8 - len(rows), LANES), jnp.float32)
        return jnp.concatenate([*rows, pad], axis=0)

    squares = jnp.zeros((vecs, LANES), jnp.float32)
    for j in range(blocks):
        raw = normals[:, block(j)]
        vq[0, :, block(j)] = raw
        value = raw.astype(jnp.float32)
        basis[0, :, block(j)] = value
        squares = squares + lane_sums(value * value)
        for m in range(1, ITERS):
            basis[m, :, block(j)] = jnp.zeros_like(value)
    start_message = message(as_row(squares, squares))

    @pl.when(me == 0)
    def _():
        prev[...] = jnp.zeros_like(prev)

    @pl.when(me == n - 1)
    def _():
        reach_r[...] = jnp.zeros_like(reach_r)

    pl.semaphore_wait(barrier, n - 1)
    send_message(ITERS, start_message)

    @pl.when(me < n - 1)
    def _():
        halo_copy(0).start()

    codes = [(ids[s, 0] - me * blocks) * band + (ids[s, 0] - ids[s, 1]) for s in range(slots)]

    def locate(p, carry):
        slot, live = jnp.int32(0), jnp.float32(0)
        for s, code in enumerate(codes):
            slot = jnp.where(code == p, jnp.int32(s), slot)
            live = jnp.where(code == p, jnp.float32(1), live)
        slot_map[p] = slot
        live_map[p] = live
        return carry

    lax.fori_loop(0, blocks * band, locate, 0)

    def product(left, i, offset, transposed):
        p = i * band + offset
        return dot(left, tiles_v[slot_map[p]], transposed) * live_map[p]

    for s in range(slots):
        tile_copy(s).wait()

    def normalise(k, eps):
        row = jnp.sqrt(total_message(ITERS + k)[0:1] + eps)
        inverse = wide(1.0 / as_columns(row)[:vecs])
        for j in range(blocks):
            basis[k, :, block(j)] = basis[k, :, block(j)] * inverse
        pltpu.make_async_copy(basis.at[k], basis_out.at[k], out_sem.at[k]).start()
        return row, inverse

    def step(k, carry):
        for c in range(blocks):
            total = None
            for i in range(c + 1):
                term = product(vq[k, :, block(i)], i, i + blocks - c, False)
                total = term if total is None else total + term
            reach_s[k, :, block(c)] = total.astype(jnp.bfloat16)

        @pl.when(me > 0)
        def _():
            back_copy(k).start()

        for j in range(blocks):
            total = None
            for i in range(j, blocks):
                term = product(vq[k, :, block(i)], i, i - j, False)
                total = term if total is None else total + term
            for c in range(j + 1):
                total = total + product(vq[k, :, block(c)], j, j - c, True)
            image[:, block(j)] = total

        row, inverse = normalise(k, jnp.where(k == 0, 0.0, EPS))

        @pl.when(k > 0)
        def _():
            betas[pl.ds(jnp.maximum(k - 1, 0), 1), :] = row[:, :vecs]

        @pl.when(me > 0)
        def _():
            halo_copy(k).wait_recv()

        for j in range(blocks):
            total = image[:, block(j)]
            for c in range(j, blocks):
                total = total + product(prev[k, :, block(c)], j, j + blocks - c, True)
            image[:, block(j)] = total

        @pl.when(me < n - 1)
        def _():
            back_copy(k).wait_recv()

        parts = [jnp.zeros((vecs, LANES), jnp.float32) for _ in range(ITERS)]
        for j in range(blocks):
            value = (image[:, block(j)] + reach_r[k, :, block(j)].astype(jnp.float32)) * inverse
            value = value + variance[:, block(j)] * basis[k, :, block(j)]
            image[:, block(j)] = value
            for m in range(ITERS):
                parts[m] = parts[m] + lane_sums(basis[m, :, block(j)] * value)
        send_message(k, message(as_row(parts[0], parts[1]), as_row(parts[2], parts[2])))
        sums = total_message(k)
        low, high = as_columns(sums[0:1]), as_columns(sums[1:2])
        proj = [wide(low[:vecs]), wide(low[vecs : 2 * vecs]), wide(high[:vecs])]
        chosen = jnp.where(k == 0, sums[0:1, :vecs], jnp.where(k == 1, sums[0:1, vecs : 2 * vecs], sums[1:2, :vecs]))
        alphas[pl.ds(k, 1), :] = chosen
        squares = jnp.zeros((vecs, LANES), jnp.float32)
        for j in range(blocks):
            value = image[:, block(j)]
            lost = basis[0, :, block(j)] * proj[0]
            for m in range(1, ITERS):
                lost = lost + basis[m, :, block(j)] * proj[m]
            value = value - lost
            basis[k + 1, :, block(j)] = value
            vq[k + 1, :, block(j)] = value.astype(jnp.bfloat16)
            squares = squares + lane_sums(value * value)

        @pl.when((k < ITERS - 1) & (me < n - 1))
        def _():
            halo_copy(k + 1).start()

        send_message(ITERS + k + 1, message(as_row(squares, squares)))
        return carry

    lax.fori_loop(0, ITERS, step, 0)
    row, _ = normalise(ITERS, EPS)
    betas[ITERS - 1 : ITERS, :] = row[:, :vecs]

    for k in range(ITERS):
        @pl.when(me < n - 1)
        def _():
            halo_copy(k).wait_send()

        @pl.when(me > 0)
        def _():
            back_copy(k).wait_send()

    for e in range(2 * ITERS + 1):
        finish_message(e)
    for k in range(ITERS + 1):
        pltpu.make_async_copy(basis.at[k], basis_out.at[k], out_sem.at[k]).wait()


def shards(n, normals, variance, tiles, tile_ids):
    vecs, sites = normals.shape
    slots, width, _ = tiles.shape
    band = sites // width + 1
    places = band * (sites // width)
    messages = 2 * ITERS + 1
    vmem = pl.BlockSpec(memory_space=pltpu.VMEM)
    any_space = pl.BlockSpec(memory_space=pl.ANY)
    dma = pltpu.SemaphoreType.DMA
    basis, alphas, betas = pl.pallas_call(
        functools.partial(kernel, n),
        out_shape=(
            jax.ShapeDtypeStruct((ITERS + 1, vecs, sites), jnp.float32),
            jax.ShapeDtypeStruct((ITERS, vecs), jnp.float32),
            jax.ShapeDtypeStruct((ITERS, vecs), jnp.float32),
        ),
        in_specs=[pl.BlockSpec(memory_space=pltpu.SMEM), vmem, vmem, any_space],
        out_specs=(any_space, vmem, vmem),
        scratch_shapes=[
            pltpu.VMEM((slots, width, width), jnp.bfloat16),
            pltpu.VMEM((ITERS + 1, vecs, sites), jnp.bfloat16),
            pltpu.VMEM((ITERS, vecs, sites), jnp.bfloat16),
            pltpu.VMEM((ITERS, vecs, sites), jnp.bfloat16),
            pltpu.VMEM((ITERS, vecs, sites), jnp.bfloat16),
            pltpu.VMEM((ITERS + 1, vecs, sites), jnp.float32),
            pltpu.VMEM((vecs, sites), jnp.float32),
            pltpu.VMEM((messages, 8, LANES), jnp.float32),
            pltpu.VMEM((messages, n, 8, LANES), jnp.float32),
            pltpu.SMEM((places,), jnp.int32),
            pltpu.SMEM((places,), jnp.float32),
            dma((slots,)),
            dma((ITERS,)),
            dma((ITERS,)),
            dma((ITERS,)),
            dma((ITERS,)),
            dma((messages,)),
            dma((messages,)),
            dma((ITERS + 1,)),
        ],
        compiler_params=pltpu.CompilerParams(
            collective_id=0, has_side_effects=True, vmem_limit_bytes=48 * 1024 * 1024
        ),
    )(tile_ids, normals, variance[None, :], tiles)
    return basis * math.sqrt(sites * n), alphas, betas


def solution(mesh):
    return jax.shard_map(
        functools.partial(shards, mesh.shape["row"]),
        mesh=mesh,
        in_specs=(
            P("groups", "row"),
            P(("groups", "row")),
            P(("groups", "row"), None, None),
            P(("groups", "row"), None),
        ),
        out_specs=(P(None, "groups", "row"), P(None, "groups"), P(None, "groups")),
        check_vma=False,
    )
```

time: 387 us -> 60.7 us (0.16)
  blocking collectives: 220 us -> 0 us
  other arithmetic: 57.6 us -> 1.5 us
  Pallas kernels: 0 us -> 54.7 us
  matrix products: 36.4 us -> 0 us
  loops' own time: 36 us -> 0 us
  local copies, waits for them, and re-layouts: 22.5 us -> 3.57 us
  starting transfers between devices: 11.2 us -> 0 us
    psum x7 -> x0, blocking collectives: 220 us -> none  [the longest x3 96.9 us: shards(): proj = lax.psum(local_proj, 'row')]
    pallas_call x0 -> x1, Pallas kernels: none -> 54.7 us  [shards(): pl.pallas_call(functools.partial(kernel, n), out_shape=(jax.ShapeDtypeStr...]
    dynamic_update_slice x20 -> x0, other arithmetic: 52.9 us -> none  [place_tile(): lax.dynamic_update_slice(cross_block, new_cross, (row_start, col_start))]
    dot_general x12 -> x0, matrix products: 36.4 us -> none  [the longest x6 16.1 us: times_transpose(): lax.dot_general(vq, block, (((1,), (1,)), ((), ())), preferred_element_ty...]
    another operation x1 -> x0, loops' own time: 36 us -> none  [build_blocks(): return lax.fori_loop(0, tiles.shape[0], place_tile, (empty, empty))]
    ppermute x6 -> x0, starting transfers between devices: 11.2 us -> none  [passed_along(): lax.ppermute(value, axis, [(source, source + steps) for source in range(l...]
    slice x22 -> x0, local copies, waits for them, and re-layouts: 10.4 us -> none  [the longest x20 10.4 us: place_tile(): col_local = slot_ids[1] - first_block]
    broadcast_in_dim x2 -> x0, local copies, waits for them, and re-layouts: 8.56 us -> none  [build_blocks(): empty = jnp.zeros((span, span), tiles.dtype)]
  transfers between devices with their start and end apart: 6 -> 0, of which waited for: 2 -> 0; matrix products, arithmetic and copies ran while one was open for 2% -> 0% of each run, Pallas kernels for 0% -> 0%
where the time goes in v1:
time: 60.7 us; the launch traced here: 60.5 us
  Pallas kernels  54.7 us (90%)
  local copies, waits for them, and re-layouts  3.57 us (6%)
  other arithmetic  1.5 us (2%)
  between operations  0.64 us (1%)
    pallas_call x1, Pallas kernels, shards(): pl.pallas_call(functools.partial(kernel, n), out_shape=(jax.ShapeDtypeStr...  54.7 us
    unnamed x7, local copies, waits for them, and re-layouts  3.57 us
    mul x1, other arithmetic, shards(): return (basis * math.sqrt(sites * n), alphas, betas)  1.5 us

profile of v1, /device:TPU:0, one launch (start us, length us, event | category | flops | bytes accessed | tf_op | source)
XLA Modules:
  0.0 60.5 jit_solution(15488685140647968313)
XLA Ops:
  0.6 0.8 %copy.7.ids = s32[20,2]{1,0:T(8,128)S(1)} copy(s32[20,2]{0,1:T(2,128)} %param.7) | data formatting | bytes 320 | tf_op args[3]
  1.4 0.0 copy-start
  1.4 0.9 %copy-done = bf16[64,2048]{1,0:T(8,128)(2,1)S(1)} copy-done((bf16[64,2048]{1,0:T(8,128)(2,1)S(1)}, bf16[64,2048]{1,0:T(8,128)(2,1)}, u32[]{:S(2)}) %copy-start) | copy-done | bytes 262168
  2.4 0.0 copy-start.1
  2.4 0.7 %copy-done.1 = f32[2048]{0:T(1024)S(1)} copy-done((f32[2048]{0:T(1024)S(1)}, f32[2048]{0:T(1024)}, u32[]{:S(2)}) %copy-start.1) | copy-done | bytes 8216
  3.0 54.7 %shard_map.67 = (f32[4,64,2048]{2,1,0:T(8,128)S(1)}, f32[3,64]{1,0:T(4,128)S(1)}, f32[3,64]{1,0:T(4,128)S(1)}) custom-call(s32[20,2]{1,0:T(8,128)S(1)} %copy.7.ids, bf16[64,2048]{1,0:T(8,128)(2,1)S(1)} %copy-done, f32[1,2048]{1,0:T(1,128)S(1)} %bitcast.1, bf16[20,512,512]{2,1,0:T(8,128)(2,1)} %tiles.1), custom_call_target="tpu_custom_call" | custom-call | tf_op jit(solution)/shard_map/pallas_call | solution.py:262
  57.8 1.5 %broadcast_multiply_fusion = f32[4,64,2048]{2,1,0:T(8,128)} fusion(f32[4,64,2048]{2,1,0:T(8,128)S(1)} %get-tuple-element.6), kind=kLoop, calls=%fused_computation | loop fusion | flops 524288 | bytes 4194304 | tf_op jit(solution)/shard_map/mul | solution.py:296
  59.3 0.6 copy.10
  59.9 0.6 copy.11
Async XLA Ops:
  1.4 0.9 %copy-start = (bf16[64,2048]{1,0:T(8,128)(2,1)S(1)}, bf16[64,2048]{1,0:T(8,128)(2,1)}, u32[]{:S(2)}) copy-start(bf16[64,2048]{1,0:T(8,128)(2,1)} %normals.1) | copy-start | bytes 786436
  2.4 0.7 %copy-start.1 = (f32[2048]{0:T(1024)S(1)}, f32[2048]{0:T(1024)}, u32[]{:S(2)}) copy-start(f32[2048]{0:T(1024)} %param.5) | copy-start | bytes 24580

commit v2 on v1

--- a/solution.py
+++ b/solution.py
@@ -36,7 +36,7 @@
 
 def kernel(
     n, ids, normals, variance, tiles, basis_out, alphas, betas,
-    tiles_v, vq, prev, reach_s, reach_r, basis, image, psend, precv, slot_map, live_map,
+    tiles_v, vq, prev, reach_s, reach_r, basis, applied, image, coef, psend, precv, slot_map, live_map,
     tile_sem, halo_send, halo_recv, back_send, back_recv, msg_send, msg_recv, out_sem,
 ):
     me = lax.axis_index("row")
@@ -73,9 +73,10 @@
             device_id={"row": lax.rem(me + 1, n)}, device_id_type=pl.DeviceIdType.MESH,
         )
 
-    def back_copy(k):
+    def back_copy(k, c):
         return pltpu.make_async_remote_copy(
-            src_ref=reach_s.at[k], dst_ref=reach_r.at[k], send_sem=back_send.at[k], recv_sem=back_recv.at[k],
+            src_ref=reach_s.at[k, c], dst_ref=reach_r.at[k, c],
+            send_sem=back_send.at[k, c], recv_sem=back_recv.at[k, c],
             device_id={"row": lax.rem(me + n - 1, n)}, device_id_type=pl.DeviceIdType.MESH,
         )
 
@@ -105,16 +106,16 @@
         pad = jnp.zeros((8 - len(rows), LANES), jnp.float32)
         return jnp.concatenate([*rows, pad], axis=0)
 
-    squares = jnp.zeros((vecs, LANES), jnp.float32)
     for j in range(blocks):
         raw = normals[:, block(j)]
         vq[0, :, block(j)] = raw
-        value = raw.astype(jnp.float32)
-        basis[0, :, block(j)] = value
-        squares = squares + lane_sums(value * value)
-        for m in range(1, ITERS):
-            basis[m, :, block(j)] = jnp.zeros_like(value)
-    start_message = message(as_row(squares, squares))
+        basis[0, :, block(j)] = raw.astype(jnp.float32)
+    for m in range(1, ITERS):
+        basis[m] = jnp.zeros(basis.shape[1:], jnp.float32)
+    for m in range(ITERS):
+        applied[m] = jnp.zeros(applied.shape[1:], jnp.float32)
+        coef[m] = jnp.zeros(coef.shape[1:], jnp.float32)
+    coef[ITERS] = jnp.ones(coef.shape[1:], jnp.float32)
 
     @pl.when(me == 0)
     def _():
@@ -125,13 +126,12 @@
         reach_r[...] = jnp.zeros_like(reach_r)
 
     pl.semaphore_wait(barrier, n - 1)
-    send_message(ITERS, start_message)
 
     @pl.when(me < n - 1)
     def _():
         halo_copy(0).start()
 
-    codes = [(ids[s, 0] - me * blocks) * band + (ids[s, 0] - ids[s, 1]) for s in range(slots)]
+    codes = [(ids[0, s] - me * blocks) * band + (ids[0, s] - ids[1, s]) for s in range(slots)]
 
     def locate(p, carry):
         slot, live = jnp.int32(0), jnp.float32(0)
@@ -151,13 +151,43 @@
     for s in range(slots):
         tile_copy(s).wait()
 
-    def normalise(k, eps):
-        row = jnp.sqrt(total_message(ITERS + k)[0:1] + eps)
-        inverse = wide(1.0 / as_columns(row)[:vecs])
+    def write_out(k):
+        return pltpu.make_async_copy(basis.at[k], basis_out.at[k], out_sem.at[k])
+
+    def finalise(k):
+        sums = total_message(k)
+        norm = jnp.sqrt(sums[2:3] + jnp.where(k == 0, 0.0, EPS))
+        inverse = 1.0 / norm
+        second = jnp.where(lax.broadcasted_iota(jnp.int32, (1, LANES), 1) >= vecs, 1, 0)
+        near = sums[0:1] * inverse * jnp.where(second == k, inverse, 1.0)
+        far = sums[1:2] * inverse * jnp.where(second + 2 == k, inverse, 1.0)
+        low, high = as_columns(near), as_columns(far)
+        columns = [low[:vecs], low[vecs : 2 * vecs], high[:vecs], as_columns(inverse)[:vecs]]
+        for m, column in enumerate(columns):
+            coef[m] = column
+        alphas[pl.ds(k, 1), :] = jnp.where(
+            k == 0, near[:, :vecs], jnp.where(k == 1, near[:, vecs : 2 * vecs], far[:, :vecs])
+        )
+
+        @pl.when(k > 0)
+        def _():
+            betas[pl.ds((k + ITERS - 1) % ITERS, 1), :] = norm[:, :vecs]
+
+        proj = [wide(column) for column in columns]
+        squares = jnp.zeros((vecs, LANES), jnp.float32)
         for j in range(blocks):
-            basis[k, :, block(j)] = basis[k, :, block(j)] * inverse
-        pltpu.make_async_copy(basis.at[k], basis_out.at[k], out_sem.at[k]).start()
-        return row, inverse
+            vector = basis[k, :, block(j)] * proj[ITERS]
+            basis[k, :, block(j)] = vector
+            product_part = applied[k, :, block(j)] * proj[ITERS]
+            applied[k, :, block(j)] = product_part
+            lost = basis[0, :, block(j)] * proj[0]
+            for m in range(1, ITERS):
+                lost = lost + basis[m, :, block(j)] * proj[m]
+            value = variance[:, block(j)] * vector + product_part - lost
+            basis[k + 1, :, block(j)] = value
+            squares = squares + lane_sums(value * value)
+        write_out(k).start()
+        return squares
 
     def step(k, carry):
         for c in range(blocks):
@@ -165,11 +195,11 @@
             for i in range(c + 1):
                 term = product(vq[k, :, block(i)], i, i + blocks - c, False)
                 total = term if total is None else total + term
-            reach_s[k, :, block(c)] = total.astype(jnp.bfloat16)
-
-        @pl.when(me > 0)
-        def _():
-            back_copy(k).start()
+            reach_s[k, c] = total.astype(jnp.bfloat16)
+
+            @pl.when(me > 0)
+            def _():
+                back_copy(k, c).start()
 
         for j in range(blocks):
             total = None
@@ -180,11 +210,9 @@
                 total = total + product(vq[k, :, block(c)], j, j - c, True)
             image[:, block(j)] = total
 
-        row, inverse = normalise(k, jnp.where(k == 0, 0.0, EPS))
-
         @pl.when(k > 0)
         def _():
-            betas[pl.ds(jnp.maximum(k - 1, 0), 1), :] = row[:, :vecs]
+            finalise(jnp.maximum(k - 1, 0))
 
         @pl.when(me > 0)
         def _():
@@ -196,44 +224,41 @@
                 total = total + product(prev[k, :, block(c)], j, j + blocks - c, True)
             image[:, block(j)] = total
 
-        @pl.when(me < n - 1)
-        def _():
-            back_copy(k).wait_recv()
-
-        parts = [jnp.zeros((vecs, LANES), jnp.float32) for _ in range(ITERS)]
+        parts = [jnp.zeros((vecs, LANES), jnp.float32) for _ in range(ITERS + 1)]
+        proj = [wide(coef[m]) for m in range(ITERS + 1)]
         for j in range(blocks):
-            value = (image[:, block(j)] + reach_r[k, :, block(j)].astype(jnp.float32)) * inverse
-            value = value + variance[:, block(j)] * basis[k, :, block(j)]
-            image[:, block(j)] = value
+            @pl.when(me < n - 1)
+            def _():
+                back_copy(k, j).wait_recv()
+
+            value = (image[:, block(j)] + reach_r[k, j].astype(jnp.float32)) * proj[ITERS]
+            for m in range(ITERS):
+                value = value - applied[m, :, block(j)] * proj[m]
+            applied[k, :, block(j)] = value
+            vector = basis[k, :, block(j)]
+            value = value + variance[:, block(j)] * vector
+            vq[k + 1, :, block(j)] = value.astype(jnp.bfloat16)
             for m in range(ITERS):
                 parts[m] = parts[m] + lane_sums(basis[m, :, block(j)] * value)
-        send_message(k, message(as_row(parts[0], parts[1]), as_row(parts[2], parts[2])))
-        sums = total_message(k)
-        low, high = as_columns(sums[0:1]), as_columns(sums[1:2])
-        proj = [wide(low[:vecs]), wide(low[vecs : 2 * vecs]), wide(high[:vecs])]
-        chosen = jnp.where(k == 0, sums[0:1, :vecs], jnp.where(k == 1, sums[0:1, vecs : 2 * vecs], sums[1:2, :vecs]))
-        alphas[pl.ds(k, 1), :] = chosen
-        squares = jnp.zeros((vecs, LANES), jnp.float32)
-        for j in range(blocks):
-            value = image[:, block(j)]
-            lost = basis[0, :, block(j)] * proj[0]
-            for m in range(1, ITERS):
-                lost = lost + basis[m, :, block(j)] * proj[m]
-            value = value - lost
-            basis[k + 1, :, block(j)] = value
-            vq[k + 1, :, block(j)] = value.astype(jnp.bfloat16)
-            squares = squares + lane_sums(value * value)
+            parts[ITERS] = parts[ITERS] + lane_sums(vector * vector)
+        last = parts[ITERS]
+        send_message(k, message(as_row(parts[0], parts[1]), as_row(parts[2], last), as_row(last, last)))
 
         @pl.when((k < ITERS - 1) & (me < n - 1))
         def _():
             halo_copy(k + 1).start()
 
-        send_message(ITERS + k + 1, message(as_row(squares, squares)))
         return carry
 
     lax.fori_loop(0, ITERS, step, 0)
-    row, _ = normalise(ITERS, EPS)
+    squares = finalise(ITERS - 1)
+    send_message(ITERS, message(as_row(squares, squares)))
+    row = jnp.sqrt(total_message(ITERS)[0:1] + EPS)
     betas[ITERS - 1 : ITERS, :] = row[:, :vecs]
+    inverse = wide(1.0 / as_columns(row)[:vecs])
+    for j in range(blocks):
+        basis[ITERS, :, block(j)] = basis[ITERS, :, block(j)] * inverse
+    write_out(ITERS).start()
 
     for k in range(ITERS):
         @pl.when(me < n - 1)
@@ -242,12 +267,13 @@
 
         @pl.when(me > 0)
         def _():
-            back_copy(k).wait_send()
-
-    for e in range(2 * ITERS + 1):
+            for c in range(blocks):
+                back_copy(k, c).wait_send()
+
+    for e in range(ITERS + 1):
         finish_message(e)
     for k in range(ITERS + 1):
-        pltpu.make_async_copy(basis.at[k], basis_out.at[k], out_sem.at[k]).wait()
+        write_out(k).wait()
 
 
 def shards(n, normals, variance, tiles, tile_ids):
@@ -255,7 +281,7 @@
     slots, width, _ = tiles.shape
     band = sites // width + 1
     places = band * (sites // width)
-    messages = 2 * ITERS + 1
+    messages = ITERS + 1
     vmem = pl.BlockSpec(memory_space=pltpu.VMEM)
     any_space = pl.BlockSpec(memory_space=pl.ANY)
     dma = pltpu.SemaphoreType.DMA
@@ -272,10 +298,12 @@
             pltpu.VMEM((slots, width, width), jnp.bfloat16),
             pltpu.VMEM((ITERS + 1, vecs, sites), jnp.bfloat16),
             pltpu.VMEM((ITERS, vecs, sites), jnp.bfloat16),
-            pltpu.VMEM((ITERS, vecs, sites), jnp.bfloat16),
-            pltpu.VMEM((ITERS, vecs, sites), jnp.bfloat16),
+            pltpu.VMEM((ITERS, sites // width, vecs, width), jnp.bfloat16),
+            pltpu.VMEM((ITERS, sites // width, vecs, width), jnp.bfloat16),
             pltpu.VMEM((ITERS + 1, vecs, sites), jnp.float32),
+            pltpu.VMEM((ITERS, vecs, sites), jnp.float32),
             pltpu.VMEM((vecs, sites), jnp.float32),
+            pltpu.VMEM((ITERS + 1, vecs, LANES), jnp.float32),
             pltpu.VMEM((messages, 8, LANES), jnp.float32),
             pltpu.VMEM((messages, n, 8, LANES), jnp.float32),
             pltpu.SMEM((places,), jnp.int32),
@@ -283,8 +311,8 @@
             dma((slots,)),
             dma((ITERS,)),
             dma((ITERS,)),
-            dma((ITERS,)),
-            dma((ITERS,)),
+            dma((ITERS, sites // width)),
+            dma((ITERS, sites // width)),
             dma((messages,)),
             dma((messages,)),
             dma((ITERS + 1,)),
@@ -292,7 +320,7 @@
         compiler_params=pltpu.CompilerParams(
             collective_id=0, has_side_effects=True, vmem_limit_bytes=48 * 1024 * 1024
         ),
-    )(tile_ids, normals, variance[None, :], tiles)
+    )(tile_ids.T, normals, variance[None, :], tiles)
     return basis * math.sqrt(sites * n), alphas, betas
 
 

time: 60.7 us -> 47.9 us (0.79)
  Pallas kernels: 54.7 us -> 42 us
    pallas_call x1, Pallas kernels: 54.7 us -> 42 us  [shards(): pl.pallas_call(functools.partial(kernel, n), out_shape=(jax.ShapeDtypeStr...]
    unnamed x7 -> x8, local copies, waits for them, and re-layouts: 3.57 us -> 3.47 us
where the time goes in v2:
time: 47.9 us; the launch traced here: 47.6 us
  Pallas kernels  42 us (88%)
  local copies, waits for them, and re-layouts  3.47 us (7%)
  other arithmetic  1.5 us (3%)
  between operations  0.65 us (1%)
    pallas_call x1, Pallas kernels, shards(): pl.pallas_call(functools.partial(kernel, n), out_shape=(jax.ShapeDtypeStr...  42 us
    unnamed x8, local copies, waits for them, and re-layouts  3.47 us
    mul x1, other arithmetic, shards(): return (basis * math.sqrt(sites * n), alphas, betas)  1.5 us

profile of v2, /device:TPU:0, one launch (start us, length us, event | category | flops | bytes accessed | tf_op | source)
XLA Modules:
  0.0 47.6 jit_solution(5611019268303389808)
XLA Ops:
  0.6 0.0 copy-start
  0.6 0.9 %copy-done = bf16[64,2048]{1,0:T(8,128)(2,1)S(1)} copy-done((bf16[64,2048]{1,0:T(8,128)(2,1)S(1)}, bf16[64,2048]{1,0:T(8,128)(2,1)}, u32[]{:S(2)}) %copy-start) | copy-done | bytes 262168
  1.6 0.0 copy-start.1
  1.6 0.7 %copy-done.1 = f32[2048]{0:T(1024)S(1)} copy-done((f32[2048]{0:T(1024)S(1)}, f32[2048]{0:T(1024)}, u32[]{:S(2)}) %copy-start.1) | copy-done | bytes 8216
  2.3 0.0 copy-start.2
  2.3 0.7 %copy-done.2 = s32[20,2]{0,1:T(2,128)S(1)} copy-done((s32[20,2]{0,1:T(2,128)S(1)}, s32[20,2]{0,1:T(2,128)}, u32[]{:S(2)}) %copy-start.2) | copy-done | bytes 184
  3.0 42.0 %shard_map.67 = (f32[4,64,2048]{2,1,0:T(8,128)S(1)}, f32[3,64]{1,0:T(4,128)S(1)}, f32[3,64]{1,0:T(4,128)S(1)}) custom-call(s32[2,20]{1,0:T(2,128)S(1)} %bitcast.3, bf16[64,2048]{1,0:T(8,128)(2,1)S(1)} %copy-done, f32[1,2048]{1,0:T(1,128)S(1)} %bitcast.2, bf16[20,512,512]{2,1,0:T(8,128)(2,1)} %tiles.1), custom_call_target="tpu_custom_call" | custom-call | tf_op jit(solution)/shard_map/pallas_call | solution.py:288
  45.0 1.5 %broadcast_multiply_fusion = f32[4,64,2048]{2,1,0:T(8,128)} fusion(f32[4,64,2048]{2,1,0:T(8,128)S(1)} %get-tuple-element.6), kind=kLoop, calls=%fused_computation | loop fusion | flops 524288 | bytes 4194304 | tf_op jit(solution)/shard_map/mul | solution.py:324
  46.5 0.6 %copy.9 = f32[3,64]{1,0:T(4,128)} copy(f32[3,64]{1,0:T(4,128)S(1)} %get-tuple-element.13) | data formatting | bytes 1536
  47.0 0.6 %copy.10 = f32[3,64]{1,0:T(4,128)} copy(f32[3,64]{1,0:T(4,128)S(1)} %get-tuple-element.14) | data formatting | bytes 1536
Async XLA Ops:
  0.6 1.0 %copy-start = (bf16[64,2048]{1,0:T(8,128)(2,1)S(1)}, bf16[64,2048]{1,0:T(8,128)(2,1)}, u32[]{:S(2)}) copy-start(bf16[64,2048]{1,0:T(8,128)(2,1)} %normals.1) | copy-start | bytes 786436
  1.6 0.7 %copy-start.1 = (f32[2048]{0:T(1024)S(1)}, f32[2048]{0:T(1024)}, u32[]{:S(2)}) copy-start(f32[2048]{0:T(1024)} %param.5) | copy-start | bytes 24580
  2.3 0.7 %copy-start.2 = (s32[20,2]{0,1:T(2,128)S(1)}, s32[20,2]{0,1:T(2,128)}, u32[]{:S(2)}) copy-start(s32[20,2]{0,1:T(2,128)} %param.7) | copy-start | bytes 484

commit v3 on v2

--- a/solution.py
+++ b/solution.py
@@ -35,19 +35,23 @@
 
 
 def kernel(
-    n, ids, normals, variance, tiles, basis_out, alphas, betas,
-    tiles_v, vq, prev, reach_s, reach_r, basis, applied, image, coef, psend, precv, slot_map, live_map,
-    tile_sem, halo_send, halo_recv, back_send, back_recv, msg_send, msg_recv, out_sem,
+    n, ids, normals_in, variance_in, tiles, basis_out, alphas, betas,
+    normals, variance, tiles_v, vq, prev, reach_s, reach_r, basis, applied, image, coef, psend, precv, slot_map, live_map,
+    tile_sem, halo_send, halo_recv, back_send, back_recv, msg_send, msg_recv, out_sem, in_sem,
 ):
     me = lax.axis_index("row")
     slots, width, _ = tiles.shape
-    vecs, sites = normals.shape
+    vecs, sites = normals_in.shape
     blocks = sites // width
     band = blocks + 1
 
     def tile_copy(s):
         return pltpu.make_async_copy(tiles.at[s], tiles_v.at[s], tile_sem.at[s])
 
+    draws_copy = pltpu.make_async_copy(normals_in, normals, in_sem.at[0])
+    variance_copy = pltpu.make_async_copy(variance_in, variance, in_sem.at[1])
+    draws_copy.start()
+    variance_copy.start()
     for s in range(slots):
         tile_copy(s).start()
 
@@ -105,6 +109,9 @@
     def message(*rows):
         pad = jnp.zeros((8 - len(rows), LANES), jnp.float32)
         return jnp.concatenate([*rows, pad], axis=0)
+
+    draws_copy.wait()
+    variance_copy.wait()
 
     for j in range(blocks):
         raw = normals[:, block(j)]
@@ -292,9 +299,11 @@
             jax.ShapeDtypeStruct((ITERS, vecs), jnp.float32),
             jax.ShapeDtypeStruct((ITERS, vecs), jnp.float32),
         ),
-        in_specs=[pl.BlockSpec(memory_space=pltpu.SMEM), vmem, vmem, any_space],
+        in_specs=[pl.BlockSpec(memory_space=pltpu.SMEM), any_space, any_space, any_space],
         out_specs=(any_space, vmem, vmem),
         scratch_shapes=[
+            pltpu.VMEM((vecs, sites), jnp.bfloat16),
+            pltpu.VMEM((1, sites), jnp.float32),
             pltpu.VMEM((slots, width, width), jnp.bfloat16),
             pltpu.VMEM((ITERS + 1, vecs, sites), jnp.bfloat16),
             pltpu.VMEM((ITERS, vecs, sites), jnp.bfloat16),
@@ -316,9 +325,10 @@
             dma((messages,)),
             dma((messages,)),
             dma((ITERS + 1,)),
+            dma((2,)),
         ],
         compiler_params=pltpu.CompilerParams(
-            collective_id=0, has_side_effects=True, vmem_limit_bytes=48 * 1024 * 1024
+            collective_id=0, has_side_effects=True, vmem_limit_bytes=62 * 1024 * 1024
         ),
     )(tile_ids.T, normals, variance[None, :], tiles)
     return basis * math.sqrt(sites * n), alphas, betas

time: 47.9 us -> 49.5 us (1.033)
  local copies, waits for them, and re-layouts: 3.47 us -> 1.16 us
  Pallas kernels: 42 us -> 44.3 us
  other arithmetic: 1.5 us -> 3.21 us
    unnamed x8 -> x6, local copies, waits for them, and re-layouts: 3.47 us -> 1.16 us
    pallas_call x1, Pallas kernels: 42 us -> 44.3 us  [shards(): pl.pallas_call(functools.partial(kernel, n), out_shape=(jax.ShapeDtypeStr...]
    mul x1, other arithmetic: 1.5 us -> 3.21 us  [shards(): return (basis * math.sqrt(sites * n), alphas, betas)]
where the time goes in v3:
time: 49.5 us; the launch traced here: 49.3 us
  Pallas kernels  44.3 us (89%)
  other arithmetic  3.21 us (6%)
  local copies, waits for them, and re-layouts  1.16 us (2%)
  between operations  0.66 us (1%)
    pallas_call x1, Pallas kernels, shards(): pl.pallas_call(functools.partial(kernel, n), out_shape=(jax.ShapeDtypeStr...  44.3 us
    mul x1, other arithmetic, shards(): return (basis * math.sqrt(sites * n), alphas, betas)  3.21 us
    unnamed x6, local copies, waits for them, and re-layouts  1.16 us

profile of v3, /device:TPU:0, one launch (start us, length us, event | category | flops | bytes accessed | tf_op | source)
XLA Modules:
  0.0 49.3 jit_solution(13108072649183922453)
XLA Ops:
  0.6 44.3 %shard_map.67 = (f32[4,64,2048]{2,1,0:T(8,128)}, f32[3,64]{1,0:T(4,128)}, f32[3,64]{1,0:T(4,128)}) custom-call(s32[2,20]{1,0:T(2,128)} %bitcast.3, bf16[64,2048]{1,0:T(8,128)(2,1)} %normals_in.1, f32[1,2048]{1,0:T(1,128)} %bitcast.2, bf16[20,512,512]{2,1,0:T(8,128)(2,1)} %tiles.1), custom_call_target="tpu_custom_call" | custom-call | tf_op jit(solution)/shard_map/pallas_call | solution.py:295
  44.9 0.0 copy-start.1
  44.9 0.0 copy-start
  44.9 3.2 %broadcast_multiply_fusion = f32[4,64,2048]{2,1,0:T(8,128)} fusion(f32[4,64,2048]{2,1,0:T(8,128)} %get-tuple-element.6), kind=kLoop, calls=%fused_computation | loop fusion | flops 524288 | bytes 4194304 | tf_op jit(solution)/shard_map/mul | solution.py:334
  48.1 0.0 copy-done.1
  48.1 0.6 %copy.9 = f32[3,64]{1,0:T(4,128)} copy(f32[3,64]{1,0:T(4,128)S(1)} %copy-done.1) | data formatting | bytes 1536
  48.7 0.0 copy-done
  48.7 0.6 %copy.10 = f32[3,64]{1,0:T(4,128)} copy(f32[3,64]{1,0:T(4,128)S(1)} %copy-done) | data formatting | bytes 1536
Async XLA Ops:
  44.9 3.2 %copy-start.1 = (f32[3,64]{1,0:T(4,128)S(1)}, f32[3,64]{1,0:T(4,128)}, u32[]{:S(2)}) copy-start(f32[3,64]{1,0:T(4,128)} %get-tuple-element.13) | copy-start | bytes 2308
  44.9 3.8 %copy-start = (f32[3,64]{1,0:T(4,128)S(1)}, f32[3,64]{1,0:T(4,128)}, u32[]{:S(2)}) copy-start(f32[3,64]{1,0:T(4,128)} %get-tuple-element.14) | copy-start | bytes 2308

commit v4 on v2

--- a/solution.py
+++ b/solution.py
@@ -241,12 +241,12 @@
             for m in range(ITERS):
                 parts[m] = parts[m] + lane_sums(basis[m, :, block(j)] * value)
             parts[ITERS] = parts[ITERS] + lane_sums(vector * vector)
+        @pl.when((k < ITERS - 1) & (me < n - 1))
+        def _():
+            halo_copy(k + 1).start()
+
         last = parts[ITERS]
         send_message(k, message(as_row(parts[0], parts[1]), as_row(parts[2], last), as_row(last, last)))
-
-        @pl.when((k < ITERS - 1) & (me < n - 1))
-        def _():
-            halo_copy(k + 1).start()
 
         return carry
 

time: 47.9 us -> 48.9 us (1.021)
  Pallas kernels: 42 us -> 43 us
    pallas_call x1, Pallas kernels: 42 us -> 43 us  [shards(): pl.pallas_call(functools.partial(kernel, n), out_shape=(jax.ShapeDtypeStr...]
where the time goes in v4:
time: 48.9 us; the launch traced here: 48.6 us
  Pallas kernels  43 us (88%)
  local copies, waits for them, and re-layouts  3.47 us (7%)
  other arithmetic  1.5 us (3%)
  between operations  0.65 us (1%)
    pallas_call x1, Pallas kernels, shards(): pl.pallas_call(functools.partial(kernel, n), out_shape=(jax.ShapeDtypeStr...  43 us
    unnamed x8, local copies, waits for them, and re-layouts  3.47 us
    mul x1, other arithmetic, shards(): return (basis * math.sqrt(sites * n), alphas, betas)  1.5 us

profile of v4, /device:TPU:0, one launch (start us, length us, event | category | flops | bytes accessed | tf_op | source)
XLA Modules:
  0.0 48.6 jit_solution(3516276057727854830)
XLA Ops:
  0.6 0.0 copy-start
  0.6 0.9 %copy-done = bf16[64,2048]{1,0:T(8,128)(2,1)S(1)} copy-done((bf16[64,2048]{1,0:T(8,128)(2,1)S(1)}, bf16[64,2048]{1,0:T(8,128)(2,1)}, u32[]{:S(2)}) %copy-start) | copy-done | bytes 262168
  1.6 0.0 copy-start.1
  1.6 0.7 %copy-done.1 = f32[2048]{0:T(1024)S(1)} copy-done((f32[2048]{0:T(1024)S(1)}, f32[2048]{0:T(1024)}, u32[]{:S(2)}) %copy-start.1) | copy-done | bytes 8216
  2.3 0.0 copy-start.2
  2.3 0.7 %copy-done.2 = s32[20,2]{0,1:T(2,128)S(1)} copy-done((s32[20,2]{0,1:T(2,128)S(1)}, s32[20,2]{0,1:T(2,128)}, u32[]{:S(2)}) %copy-start.2) | copy-done | bytes 184
  3.0 43.0 %shard_map.67 = (f32[4,64,2048]{2,1,0:T(8,128)S(1)}, f32[3,64]{1,0:T(4,128)S(1)}, f32[3,64]{1,0:T(4,128)S(1)}) custom-call(s32[2,20]{1,0:T(2,128)S(1)} %bitcast.3, bf16[64,2048]{1,0:T(8,128)(2,1)S(1)} %copy-done, f32[1,2048]{1,0:T(1,128)S(1)} %bitcast.2, bf16[20,512,512]{2,1,0:T(8,128)(2,1)} %tiles.1), custom_call_target="tpu_custom_call" | custom-call | tf_op jit(solution)/shard_map/pallas_call | solution.py:288
  46.0 1.5 %broadcast_multiply_fusion = f32[4,64,2048]{2,1,0:T(8,128)} fusion(f32[4,64,2048]{2,1,0:T(8,128)S(1)} %get-tuple-element.6), kind=kLoop, calls=%fused_computation | loop fusion | flops 524288 | bytes 4194304 | tf_op jit(solution)/shard_map/mul | solution.py:324
  47.5 0.6 %copy.9 = f32[3,64]{1,0:T(4,128)} copy(f32[3,64]{1,0:T(4,128)S(1)} %get-tuple-element.13) | data formatting | bytes 1536
  48.1 0.6 %copy.10 = f32[3,64]{1,0:T(4,128)} copy(f32[3,64]{1,0:T(4,128)S(1)} %get-tuple-element.14) | data formatting | bytes 1536
Async XLA Ops:
  0.6 1.0 %copy-start = (bf16[64,2048]{1,0:T(8,128)(2,1)S(1)}, bf16[64,2048]{1,0:T(8,128)(2,1)}, u32[]{:S(2)}) copy-start(bf16[64,2048]{1,0:T(8,128)(2,1)} %normals.1) | copy-start | bytes 786436
  1.6 0.7 %copy-start.1 = (f32[2048]{0:T(1024)S(1)}, f32[2048]{0:T(1024)}, u32[]{:S(2)}) copy-start(f32[2048]{0:T(1024)} %param.5) | copy-start | bytes 24580
  2.3 0.7 %copy-start.2 = (s32[20,2]{0,1:T(2,128)S(1)}, s32[20,2]{0,1:T(2,128)}, u32[]{:S(2)}) copy-start(s32[20,2]{0,1:T(2,128)} %param.7) | copy-start | bytes 484
